TPU v7x, 32 devices: a whole 2x2x4 slice. The times are simulated.
32 devices in a mesh: parts: 2 (over y), node: 4 (over z), expert: 2 (over x), rep: 2 (over core).
Axes of the slice: x: 2, y: 2, z: 4, core: 2. Of those that a mesh axis runs over, the one named last changes fastest.
Arguments:
- token_values: bfloat16 [256, 5120], P(('parts', 'node', 'expert', 'rep')), parts along dimension 0, may hold values from -6 to 6
- block_scales: bfloat16 [256, 40], P(('parts', 'node', 'expert', 'rep')), parts along dimension 0, may hold values from 0.25 to 4
- expert_ids: int32 [256, 4], P(('parts', 'node', 'expert', 'rep')), parts along dimension 0, may hold values from 0 to 7, as said below
- gate_values: bfloat16 [256, 4], P(('parts', 'node', 'expert', 'rep')), parts along dimension 0, may hold values from 0.099609375 to 1
- gate_proj: bfloat16 [8, 5120, 1024], P(('node', 'rep'), None, 'expert'), may hold values from -0.078125 to 0.078125
- up_proj: bfloat16 [8, 5120, 1024], P(('node', 'rep'), None, 'expert'), may hold values from -0.078125 to 0.078125
- down_proj: bfloat16 [8, 1024, 5120], P(('node', 'rep'), None, 'expert'), may hold values from -0.1875 to 0.1875
Outputs:
- combined: bfloat16 [256, 5120], P(('parts', 'node', 'expert', 'rep')), parts along dimension 0
There are 2 independent parts, one for each index of `parts`. A program takes and returns all parts, laid end to end along the dimension named above; an argument that names none is the same for every part. Nothing has to cross between parts.
Inputs may be any that keep to these rules, and one draw needn't show every extreme that they name: `expert_ids`: each token names 4 different experts lying in exactly 3 different node groups (expert e in group e // 2); in one of them it names both experts, in the others one. Among the 8 tokens of one device every node group is named by 6 - 1 to 6 tokens, and some group by exactly 6.
All inputs are finite; a program needn't handle non-finite values.
Results may differ from a plain program's by a relative error of at most 0.012.
Values may be sent and summed in bfloat16 or wider, within the bound.
A program may use at most 64 MiB of HBM per device.

v0:
```python
import jax
import jax.numpy as jnp
from jax import lax
from jax.sharding import PartitionSpec as P

LIMIT = 3
GROUP_EXP = 2


def dequantize(values, scales):
    lead_dims = values.shape[:-1]
    width = values.shape[-1]
    blocks = (
        values.astype(jnp.float32).reshape(lead_dims + (width // 128, 128))
        * scales.astype(jnp.float32)[..., None]
    )
    return blocks.reshape(values.shape).astype(jnp.bfloat16)


def per_device(token_values, block_scales, expert_ids, gate_values, gate_proj, up_proj, down_proj):
    groups = lax.axis_size("node")
    members = lax.axis_size("expert")
    tok_rows, width = token_values.shape
    block_count = block_scales.shape[1]
    capacity = (LIMIT * tok_rows + groups - 1) // groups
    gate_local = gate_proj[0]
    up_local = up_proj[0]
    down_local = down_proj[0]
    column_count = down_local.shape[1]
    group_index = expert_ids // GROUP_EXP
    side_index = expert_ids % GROUP_EXP
    group_hit = group_index[:, :, None] == jnp.arange(groups, dtype=jnp.int32)[None, None, :]
    in_group = jnp.any(group_hit, axis=1).astype(jnp.int32)
    ahead_count = jnp.cumsum(in_group, axis=0) - in_group
    slot_hit = (ahead_count[:, :, None] == jnp.arange(capacity, dtype=jnp.int32)[None, None, :]) & (
        in_group[:, :, None] > 0
    )
    assign = (
        jnp.transpose(slot_hit, (1, 2, 0)).reshape(groups * capacity, tok_rows).astype(jnp.bfloat16)
    )
    side_hit = (
        side_index[:, :, None] == jnp.arange(GROUP_EXP, dtype=jnp.int32)[None, None, :]
    ).astype(jnp.float32)
    pair_gates = jnp.einsum(
        "tkg,tks->tgs",
        group_hit.astype(jnp.float32),
        side_hit * gate_values.astype(jnp.float32)[:, :, None],
        precision=lax.Precision.HIGHEST,
    )
    send_gates = jnp.einsum(
        "tgc,tgs->gcs", slot_hit.astype(jnp.float32), pair_gates, precision=lax.Precision.HIGHEST
    ).astype(jnp.bfloat16)
    send_values = (
        jnp.dot(assign, token_values, preferred_element_type=jnp.float32)
        .astype(jnp.bfloat16)
        .reshape(groups, capacity, width)
    )
    send_scales = (
        jnp.dot(assign, block_scales, preferred_element_type=jnp.float32)
        .astype(jnp.bfloat16)
        .reshape(groups, capacity, block_count)
    )
    spread_values = jnp.broadcast_to(
        send_values[:, None], (groups, members, capacity, width)
    ).reshape(groups * members, capacity, width)
    spread_scales = jnp.broadcast_to(
        send_scales[:, None], (groups, members, capacity, block_count)
    ).reshape(groups * members, capacity, block_count)
    spread_gates = jnp.broadcast_to(
        send_gates[:, None], (groups, members, capacity, GROUP_EXP)
    ).reshape(groups * members, capacity, GROUP_EXP)
    got_values, got_scales, got_gates = (
        lax.all_to_all(spread_values, ("node", "expert"), split_axis=0, concat_axis=0, tiled=True),
        lax.all_to_all(spread_scales, ("node", "expert"), split_axis=0, concat_axis=0, tiled=True),
        lax.all_to_all(spread_gates, ("node", "expert"), split_axis=0, concat_axis=0, tiled=True),
    )
    side_values = got_values.reshape(groups, members, capacity, width)
    side_scales = got_scales.reshape(groups, members, capacity, block_count)
    side_gates = got_gates.reshape(groups, members, capacity, GROUP_EXP)
    pair_values, pair_scales, pair_slot_gates = (
        lax.all_gather(side_values[None], "rep", axis=0, tiled=True),
        lax.all_gather(side_scales[None], "rep", axis=0, tiled=True),
        lax.all_gather(side_gates[None], "rep", axis=0, tiled=True),
    )
    arrived = dequantize(pair_values, pair_scales).reshape(-1, width)
    gate_part = jnp.dot(arrived, gate_local, preferred_element_type=jnp.float32)
    up_part = jnp.dot(arrived, up_local, preferred_element_type=jnp.float32)
    hidden = (jax.nn.silu(gate_part) * up_part).astype(jnp.bfloat16)
    summed = jnp.dot(
        lax.all_gather(hidden, "expert", axis=1, tiled=True),
        down_local,
        preferred_element_type=jnp.float32,
    )
    expert_out = summed.astype(jnp.bfloat16)
    own_side = (jnp.arange(GROUP_EXP, dtype=jnp.int32) == lax.axis_index("rep")).astype(jnp.float32)
    gate_mine = jnp.sum(
        pair_slot_gates.reshape(-1, GROUP_EXP).astype(jnp.float32) * own_side[None, :], axis=1
    )
    gated_out = (gate_mine[:, None] * expert_out.astype(jnp.float32)).reshape(
        GROUP_EXP, -1, column_count
    )
    group_sum = lax.psum_scatter(
        gated_out.astype(jnp.bfloat16), "rep", scatter_dimension=0, tiled=True
    )
    outputs = group_sum.reshape(groups, members, capacity, column_count)
    flat_back = lax.all_to_all(
        outputs.reshape(groups * members, capacity, column_count),
        ("node", "expert"),
        split_axis=0,
        concat_axis=0,
        tiled=True,
    )
    returned = flat_back.reshape(groups, members, capacity, column_count)
    return_table = jnp.transpose(returned, (0, 2, 1, 3)).reshape(
        groups * capacity, members * column_count
    )
    combined = jnp.dot(assign.T, return_table, preferred_element_type=jnp.float32)
    return combined.astype(jnp.bfloat16)


def solution(mesh):
    return jax.shard_map(
        per_device,
        mesh=mesh,
        in_specs=(
            P(("parts", "node", "expert", "rep"), None),
            P(("parts", "node", "expert", "rep"), None),
            P(("parts", "node", "expert", "rep"), None),
            P(("parts", "node", "expert", "rep"), None),
            P(("node", "rep"), None, "expert"),
            P(("node", "rep"), None, "expert"),
            P(("node", "rep"), None, "expert"),
        ),
        out_specs=P(("parts", "node", "expert", "rep"), None),
        check_vma=False,
    )
```

profile of v0, /device:TPU:0, one launch (start us, length us, event | category | flops | bytes accessed | tf_op | source)
XLA Modules:
  0.0 108.2 jit_solution(2833674303398674786)
XLA Ops:
  6.5 0.8 copy.74
  9.6 7.3 %all-to-all-start = ((bf16[8,6,2]{1,2,0:T(2,128)(2,1)}), bf16[8,6,2]{1,2,0:T(2,128)(2,1)S(1)}, u32[]{:S(2)}, u32[]{:S(2)}) async-start(bf16[8,6,2]{1,2,0:T(2,128)(2,1)} %copy.83), calls=%async_computation | async-start | bytes 8192 | tf_op jit(solution)/shard_map/all_to_all | solution.py:75
  17.2 0.9 convolution_convert_fusion.2
  18.1 5.1 %all-to-all-done = bf16[8,6,2]{1,2,0:T(2,128)(2,1)S(1)} async-done(((bf16[8,6,2]{1,2,0:T(2,128)(2,1)}), bf16[8,6,2]{1,2,0:T(2,128)(2,1)S(1)}, u32[]{:S(2)}, u32[]{:S(2)}) %all-to-all-start) | async-done | bytes 224 | tf_op jit(solution)/shard_map/all_to_all | solution.py:75
  23.8 3.3 %all-to-all-start.2 = ((bf16[8,6,40]{2,1,0:T(8,128)(2,1)}), bf16[8,6,40]{2,1,0:T(8,128)(2,1)S(1)}, u32[]{:S(2)}, u32[]{:S(2)}) async-start(bf16[8,6,40]{2,1,0:T(8,128)(2,1)} %bitcast.6), calls=%async_computation.2 | async-start | bytes 32768 | tf_op jit(solution)/shard_map/all_to_all | solution.py:74
  27.5 6.1 %all-to-all-done.2 = bf16[8,6,40]{2,1,0:T(8,128)(2,1)S(1)} async-done(((bf16[8,6,40]{2,1,0:T(8,128)(2,1)}), bf16[8,6,40]{2,1,0:T(8,128)(2,1)S(1)}, u32[]{:S(2)}, u32[]{:S(2)}) %all-to-all-start.2) | async-done | bytes 3872 | tf_op jit(solution)/shard_map/all_to_all | solution.py:74
  33.7 0.9 broadcast_in_dim.12
  34.6 3.5 %all-to-all-start.1 = ((bf16[8,6,5120]{2,1,0:T(8,128)(2,1)}), bf16[8,6,5120]{2,1,0:T(8,128)(2,1)S(1)}, u32[]{:S(2)}, u32[]{:S(2)}) async-start(bf16[8,6,5120]{2,1,0:T(8,128)(2,1)} %bitcast.4), calls=%async_computation.1 | async-start | bytes 1310720 | tf_op jit(solution)/shard_map/all_to_all | solution.py:73
  38.2 1.8 %all_gather.12 = bf16[2,4,2,6,2]{3,1,4,2,0:T(4,128)(2,1)S(1)} all-gather(bf16[1,4,2,6,2]{3,1,4,2,0:T(4,128)(2,1)S(1)} %copy.85), channel_id=1, replica_groups=mesh['parts'=2,'node'=4,'expert'=2,'rep'=2] {'rep'}, dimensions={0}, use_global_device_ids=true | all-gather | bytes 576 | tf_op jit(solution)/shard_map/all_gather | solution.py:83
  40.2 1.8 %all_gather.14 = bf16[2,4,2,6,40]{4,1,3,2,0:T(4,128)(2,1)S(1)} all-gather(bf16[1,4,2,6,40]{4,1,3,2,0:T(4,128)(2,1)S(1)} %copy.90), channel_id=1, replica_groups=mesh['parts'=2,'node'=4,'expert'=2,'rep'=2] {'rep'}, dimensions={0}, use_global_device_ids=true | all-gather | bytes 11520 | tf_op jit(solution)/shard_map/all_gather | solution.py:82
  42.0 1.9 %mul.51 = f32[2,4,2,6,40,128]{5,4,2,3,1,0:T(8,128)} broadcast(f32[2,4,2,6,40]{4,2,3,1,0:T(2,128)S(1)} %copy.91), dimensions={0,1,2,3,4} | broadcast | bytes 1981440 | tf_op jit(solution)/shard_map/mul | solution.py:14
  43.9 2.3 %mul.52 = f32[2,4,2,6,5120]{4,2,3,1,0:T(2,128)S(1)} reshape(f32[2,4,2,6,40,128]{5,4,2,3,1,0:T(8,128)} %mul.51) | data formatting | bytes 3932160 | tf_op jit(solution)/shard_map/mul | solution.py:14
  46.2 6.9 %all-to-all-done.1 = bf16[8,6,5120]{2,1,0:T(8,128)(2,1)S(1)} async-done(((bf16[8,6,5120]{2,1,0:T(8,128)(2,1)}), bf16[8,6,5120]{2,1,0:T(8,128)(2,1)S(1)}, u32[]{:S(2)}, u32[]{:S(2)}) %all-to-all-start.1) | async-done | bytes 491552 | tf_op jit(solution)/shard_map/all_to_all | solution.py:73
  53.5 2.5 %all_gather.13 = bf16[2,4,2,6,5120]{4,1,3,2,0:T(4,128)(2,1)S(1)} all-gather(bf16[1,4,2,6,5120]{4,1,3,2,0:T(4,128)(2,1)S(1)} %copy.88), channel_id=1, replica_groups=mesh['parts'=2,'node'=4,'expert'=2,'rep'=2] {'rep'}, dimensions={0}, use_global_device_ids=true | all-gather | bytes 1474560 | tf_op jit(solution)/shard_map/all_gather | solution.py:81
  56.0 1.6 %fusion.18 = bf16[2,4,2,6,5120]{4,1,3,2,0:T(4,128)(2,1)S(1)} fusion(f32[2,4,2,6,5120]{4,2,3,1,0:T(2,128)S(1)} %mul.52, bf16[2,4,2,6,5120]{4,1,3,2,0:T(4,128)(2,1)S(1)} %all_gather.13), kind=kLoop, calls=%fused_computation.13 | loop fusion | flops 1474560 | bytes 3932160 | tf_op jit(solution)/shard_map/convert_element_type | solution.py:17
  58.3 3.4 %fusion.4 = f32[96,512]{1,0:T(8,128)S(1)} fusion(bf16[96,5120]{1,0:T(8,128)(2,1)S(1)} %reshape.100, bf16[1,5120,512]{2,1,0:T(8,128)(2,1)} %param.11), kind=kOutput, calls=%fused_computation.6 | convolution fusion | flops 503316480 | bytes 6422528 | tf_op jit(solution)/shard_map/dot_general | solution.py:86
  61.7 3.5 %fusion.22 = bf16[96,512]{1,0:T(8,128)(2,1)S(1)} fusion(bf16[96,5120]{1,0:T(8,128)(2,1)S(1)} %reshape.100, bf16[1,5120,512]{2,1,0:T(8,128)(2,1)} %param.12, f32[96,512]{1,0:T(8,128)S(1)} %fusion.4), kind=kOutput, calls=%fused_computation.15 | convolution fusion | flops 503611392 | bytes 6520832 | tf_op jit(solution)/shard_map/dot_general | solution.py:87
  65.2 5.5 %all_gather.15 = bf16[96,1024]{1,0:T(8,128)(2,1)S(1)} all-gather(bf16[96,512]{1,0:T(8,128)(2,1)S(1)} %fusion.22), channel_id=1, replica_groups=mesh['parts'=2,'node'=4,'expert'=2,'rep'=2] {'expert'}, dimensions={1}, use_global_device_ids=true | all-gather | bytes 294912 | tf_op jit(solution)/shard_map/all_gather | solution.py:90
  70.7 4.2 %fusion.15 = bf16[96,2560]{1,0:T(8,128)(2,1)} fusion(bf16[96,1024]{1,0:T(8,128)(2,1)S(1)} %all_gather.15, bf16[1,1024,2560]{2,1,0:T(8,128)(2,1)} %param.13, f32[96]{0:T(128)S(1)} %mul.49), kind=kOutput, calls=%fused_computation.11 | convolution fusion | flops 504299520 | bytes 5931392 | tf_op jit(solution)/shard_map/dot_general | solution.py:89
  74.9 7.1 %reduce-scatter.2.cloned.1.call-done = bf16[1,48,2560]{2,1,0:T(8,128)(2,1)} async-done(((bf16[2,48,2560]{2,1,0:T(8,128)(2,1)}), bf16[1,48,2560]{2,1,0:T(8,128)(2,1)}) %reduce-scatter.2.cloned.1.call-update) | async-done | bytes 245776 | tf_op jit(solution)/shard_map/reduce_scatter | solution.py:102
  82.0 1.7 %reshape_reshape.3 = bf16[8,6,2560]{2,1,0:T(8,128)(2,1)} reshape(bf16[1,48,2560]{2,1,0:T(8,128)(2,1)} %reduce-scatter.2.cloned.1.call-done) | data formatting | bytes 491520 | tf_op jit(solution)/shard_map/reshape;reshape | solution.py:107
  83.8 5.7 %all-to-all-start.3 = ((bf16[8,6,2560]{2,1,0:T(8,128)(2,1)}), bf16[8,6,2560]{2,1,0:T(8,128)(2,1)S(1)}, u32[]{:S(2)}, u32[]{:S(2)}) async-start(bf16[8,6,2560]{2,1,0:T(8,128)(2,1)} %reshape_reshape.3), calls=%async_computation.4 | async-start | bytes 655360 | tf_op jit(solution)/shard_map/all_to_all | solution.py:106
  89.7 10.6 %all-to-all-done.3 = bf16[8,6,2560]{2,1,0:T(8,128)(2,1)S(1)} async-done(((bf16[8,6,2560]{2,1,0:T(8,128)(2,1)}), bf16[8,6,2560]{2,1,0:T(8,128)(2,1)S(1)}, u32[]{:S(2)}, u32[]{:S(2)}) %all-to-all-start.3) | async-done | bytes 245792 | tf_op jit(solution)/shard_map/all_to_all | solution.py:106
  100.5 0.8 convolution_convert_fusion.1
  (43 shorter events, 5.3 us)
Async XLA Ops:
  6.5 20.6 %copy-start = (bf16[8,5120]{1,0:T(8,128)(2,1)S(1)}, bf16[8,5120]{1,0:T(8,128)(2,1)}, u32[]{:S(2)}) copy-start(bf16[8,5120]{1,0:T(8,128)(2,1)} %param.7) | copy-start | bytes 245764
  9.6 13.6 %all-to-all-start = ((bf16[8,6,2]{1,2,0:T(2,128)(2,1)}), bf16[8,6,2]{1,2,0:T(2,128)(2,1)S(1)}, u32[]{:S(2)}, u32[]{:S(2)}) async-start(bf16[8,6,2]{1,2,0:T(2,128)(2,1)} %copy.83), calls=%async_computation | async-start | bytes 8192 | tf_op jit(solution)/shard_map/all_to_all | solution.py:75
  23.8 9.9 %all-to-all-start.2 = ((bf16[8,6,40]{2,1,0:T(8,128)(2,1)}), bf16[8,6,40]{2,1,0:T(8,128)(2,1)S(1)}, u32[]{:S(2)}, u32[]{:S(2)}) async-start(bf16[8,6,40]{2,1,0:T(8,128)(2,1)} %bitcast.6), calls=%async_computation.2 | async-start | bytes 32768 | tf_op jit(solution)/shard_map/all_to_all | solution.py:74
  34.6 18.5 %all-to-all-start.1 = ((bf16[8,6,5120]{2,1,0:T(8,128)(2,1)}), bf16[8,6,5120]{2,1,0:T(8,128)(2,1)S(1)}, u32[]{:S(2)}, u32[]{:S(2)}) async-start(bf16[8,6,5120]{2,1,0:T(8,128)(2,1)} %bitcast.4), calls=%async_computation.1 | async-start | bytes 1310720 | tf_op jit(solution)/shard_map/all_to_all | solution.py:73
  38.1 43.9 %reduce-scatter.2.cloned.1.call-start = ((), (), s32[]{:S(2)}) async-start(), calls=%async_computation.5 | async-start | bytes 737280 | tf_op jit(solution)/shard_map/reduce_scatter | solution.py:102
  83.8 16.5 %all-to-all-start.3 = ((bf16[8,6,2560]{2,1,0:T(8,128)(2,1)}), bf16[8,6,2560]{2,1,0:T(8,128)(2,1)S(1)}, u32[]{:S(2)}, u32[]{:S(2)}) async-start(bf16[8,6,2560]{2,1,0:T(8,128)(2,1)} %reshape_reshape.3), calls=%async_computation.4 | async-start | bytes 655360 | tf_op jit(solution)/shard_map/all_to_all | solution.py:106
Sparse Core Ops, SparseCore 0:
  75.1 6.9 reduce-scatter.1
where the time goes:
time: 109 us; the launch traced here: 108 us
  waiting for transfers between devices  35.8 us (33%)
  starting transfers between devices  19.9 us (18%)
  between operations  13.6 us (12%)
  matrix products  13.5 us (12%)
  local copies, waits for them, and re-layouts  11.9 us (11%)
  blocking collectives  11.6 us (11%)
  other arithmetic  1.89 us (2%)
    all_to_all x1, waiting for transfers between devices, per_device(): lax.all_to_all(outputs.reshape(groups * members, capacity, column_count),...  10.6 us
    all_to_all x1, starting transfers between devices, per_device(): lax.all_to_all(spread_gates, ('node', 'expert'), split_axis=0, concat_axi...  7.25 us
    reduce_scatter x1, waiting for transfers between devices, per_device(): lax.psum_scatter(gated_out.astype(jnp.bfloat16), 'rep', scatter_dimension...  7.1 us
    all_to_all x1, waiting for transfers between devices, per_device(): lax.all_to_all(spread_values, ('node', 'expert'), split_axis=0, concat_ax...  6.87 us
    all_to_all x1, waiting for transfers between devices, per_device(): lax.all_to_all(spread_scales, ('node', 'expert'), split_axis=0, concat_ax...  6.13 us
    all_to_all x1, starting transfers between devices, per_device(): lax.all_to_all(outputs.reshape(groups * members, capacity, column_count),...  5.74 us
    all_gather x1, blocking collectives, per_device(): lax.all_gather(hidden, 'expert', axis=1, tiled=True)  5.51 us
    all_to_all x1, waiting for transfers between devices, per_device(): lax.all_to_all(spread_gates, ('node', 'expert'), split_axis=0, concat_axi...  5.07 us
  transfers between devices with their start and end apart: 5, of which 5 were waited for; matrix products, arithmetic and copies ran while one was open for 6% of the time, Pallas kernels for 0%

commit v1 on v0

--- a/solution.py
+++ b/solution.py
@@ -1,6 +1,10 @@
+import functools
+
 import jax
 import jax.numpy as jnp
 from jax import lax
+from jax.experimental import pallas as pl
+from jax.experimental.pallas import tpu as pltpu
 from jax.sharding import PartitionSpec as P
 
 LIMIT = 3
@@ -118,9 +122,269 @@
     return combined.astype(jnp.bfloat16)
 
 
+NODES = 4
+MESH = pl.DeviceIdType.MESH
+PHASES = 2
+TILES = 2
+
+
+def fused_kernel(
+    tok_ref, scale_ref, ids_ref, gate_ref, gate_hbm, up_hbm, down_hbm, out_ref,
+    wg, wu, wd, slabs, rows, gates, acc_g, acc_u, hidden, acc_d,
+    mate_out, mate_in, back_out, back_in, final, last_out, last_in,
+    w_sem, recv_sem, z_sem, x_sem, m_sem, h_sem, r_sem, b_send, b_recv, f_sem,
+):
+    part = lax.axis_index("parts")
+    n = lax.axis_index("node")
+    e = lax.axis_index("expert")
+    r = lax.axis_index("rep")
+    width = tok_ref.shape[1]
+    half = width // 2
+    ff = wg.shape[1]
+    step = half // PHASES
+
+    weights = [
+        pltpu.make_async_copy(gate_hbm.at[0], wg, w_sem.at[0]),
+        pltpu.make_async_copy(up_hbm.at[0], wu, w_sem.at[1]),
+        pltpu.make_async_copy(down_hbm.at[0], wd, w_sem.at[2]),
+    ]
+    for copy in weights:
+        copy.start()
+
+    near = n + 1 - 2 * (n % 2)
+    peers = [near, (n + 2) % 4, 3 - n]
+    z_devs = [(part, p, e, r) for p in peers]
+    x_dev = (part, n, 1 - e, r)
+    m_dev = (part, n, e, 1 - r)
+
+    barrier = pltpu.get_barrier_semaphore()
+    for dev in z_devs + [x_dev, m_dev]:
+        pl.semaphore_signal(barrier, inc=1, device_id=dev, device_id_type=MESH)
+
+    def slot(a, b, c):
+        return (a * 2 + b) * 2 + c
+
+    me = slot(n, e, r)
+    scales = scale_ref[...].astype(jnp.float32)
+    for j in range(half // 128):
+        lo = tok_ref[:, j * 128:(j + 1) * 128].astype(jnp.float32) * scales[:, j:j + 1]
+        k = j + half // 128
+        hi = tok_ref[:, k * 128:(k + 1) * 128].astype(jnp.float32) * scales[:, k:k + 1]
+        slabs[me, :, j * 128:(j + 1) * 128] = jnp.concatenate([lo, hi], axis=0).astype(jnp.bfloat16)
+    lane = lax.broadcasted_iota(jnp.int32, (tok_ref.shape[0], 128), 1)
+    table = jnp.zeros(lane.shape, jnp.float32)
+    for k in range(ids_ref.shape[1]):
+        table = table + jnp.where(
+            ids_ref[:, k:k + 1] == lane, gate_ref[:, k:k + 1].astype(jnp.float32), 0.0
+        )
+    slabs[me, :, half:half + 128] = jnp.concatenate([table, table], axis=0).astype(jnp.bfloat16)
+
+    pl.semaphore_wait(barrier, 5)
+
+    def cols(c):
+        stop = (c + 1) * step + (128 if c == PHASES - 1 else 0)
+        return pl.ds(c * step, stop - c * step)
+
+    def send(src, c, sem, dev):
+        block = slabs.at[src, :, cols(c)]
+        copy = pltpu.make_async_remote_copy(
+            src_ref=block, dst_ref=block, send_sem=sem, recv_sem=recv_sem.at[src, c],
+            device_id=dev, device_id_type=MESH,
+        )
+        copy.start()
+        return copy
+
+    def arrive(src, c):
+        block = slabs.at[src, :, cols(c)]
+        pltpu.make_async_remote_copy(
+            src_ref=block, dst_ref=block, send_sem=m_sem.at[0, 0], recv_sem=recv_sem.at[src, c],
+            device_id=m_dev, device_id_type=MESH,
+        ).wait_recv()
+
+    sent = []
+    for c in range(PHASES):
+        for i in (2, 1, 0):
+            sent.append(send(me, c, z_sem.at[i, c], z_devs[i]))
+        sent.append(send(me, c, x_sem.at[3, c], x_dev))
+        sent.append(send(me, c, m_sem.at[3, c], m_dev))
+
+    acc_g[...] = jnp.zeros_like(acc_g)
+    acc_u[...] = jnp.zeros_like(acc_u)
+    for c in range(PHASES):
+        for i in range(3):
+            src = slot(peers[i], e, r)
+            arrive(src, c)
+            sent.append(send(src, c, x_sem.at[i, c], x_dev))
+            sent.append(send(src, c, m_sem.at[i, c], m_dev))
+        for i, p in enumerate([n] + peers):
+            src = slot(p, 1 - e, r)
+            arrive(src, c)
+            sent.append(send(src, c, m_sem.at[4 + i, c], m_dev))
+        for p in [n] + peers:
+            arrive(slot(p, e, 1 - r), c)
+            arrive(slot(p, 1 - e, 1 - r), c)
+        lo_cols = slice(c * step, (c + 1) * step)
+        hi_cols = slice(half + c * step, half + (c + 1) * step)
+        for rr in range(2):
+            for nn in range(NODES):
+                one = slabs[slot(nn, 0, rr), :, lo_cols].astype(jnp.float32)
+                two = slabs[slot(nn, 1, rr), :, lo_cols].astype(jnp.float32)
+                at = (rr * NODES + nn) * 16
+                rows[at:at + 16, lo_cols] = jnp.concatenate([one[:8], two[:8]], axis=0).astype(jnp.bfloat16)
+                rows[at:at + 16, hi_cols] = jnp.concatenate([one[8:], two[8:]], axis=0).astype(jnp.bfloat16)
+        if c == 0:
+            weights[0].wait()
+            weights[1].wait()
+        for span in (lo_cols, hi_cols):
+            acc_g[...] += jnp.dot(rows[:, span], wg[span, :], preferred_element_type=jnp.float32)
+            acc_u[...] += jnp.dot(rows[:, span], wu[span, :], preferred_element_type=jnp.float32)
+
+    gate_v = acc_g[...]
+    hidden[e] = ((gate_v / (1.0 + jnp.exp(-gate_v))) * acc_u[...]).astype(jnp.bfloat16)
+    h_copy = pltpu.make_async_remote_copy(
+        src_ref=hidden.at[e], dst_ref=hidden.at[e], send_sem=h_sem.at[0], recv_sem=h_sem.at[1],
+        device_id=x_dev, device_id_type=MESH,
+    )
+    h_copy.start()
+
+    mine = lax.broadcasted_iota(jnp.int32, (16, 128), 1) == n * 2 + r
+    for rr in range(2):
+        for nn in range(NODES):
+            one = slabs[slot(nn, 0, rr), :, half:half + 128].astype(jnp.float32)
+            two = slabs[slot(nn, 1, rr), :, half:half + 128].astype(jnp.float32)
+            both = jnp.concatenate([one[:8], two[:8]], axis=0)
+            at = (rr * NODES + nn) * 16
+            picked = jnp.sum(jnp.where(mine, both, 0.0), axis=1, keepdims=True)
+            gates[at:at + 16, :] = jnp.broadcast_to(picked, (16, 128))
+
+    weights[2].wait()
+    wide = wd.shape[1] // TILES
+    own_ff = pl.ds(pl.multiple_of(e * ff, ff), ff)
+    other_ff = pl.ds(pl.multiple_of((1 - e) * ff, ff), ff)
+    for t in range(TILES):
+        span = slice(t * wide, (t + 1) * wide)
+        acc_d[:, span] = jnp.dot(hidden[e], wd[own_ff, span], preferred_element_type=jnp.float32)
+    h_copy.wait()
+    group_rows = NODES * 16
+    own_rows = pl.ds(pl.multiple_of(r * group_rows, group_rows), group_rows)
+    mate_rows = pl.ds(pl.multiple_of((1 - r) * group_rows, group_rows), group_rows)
+    r_copies = []
+    for t in range(TILES):
+        span = slice(t * wide, (t + 1) * wide)
+        acc_d[:, span] += jnp.dot(hidden[1 - e], wd[other_ff, span], preferred_element_type=jnp.float32)
+        done = acc_d[mate_rows, span].astype(jnp.bfloat16).astype(jnp.float32)
+        mate_out[:, span] = (done * gates[mate_rows, 0:1]).astype(jnp.bfloat16)
+        copy = pltpu.make_async_remote_copy(
+            src_ref=mate_out.at[:, span], dst_ref=mate_in.at[:, span],
+            send_sem=r_sem.at[0, t], recv_sem=r_sem.at[1, t], device_id=m_dev, device_id_type=MESH,
+        )
+        copy.start()
+        r_copies.append(copy)
+    b_copies = []
+    for t in range(TILES):
+        span = slice(t * wide, (t + 1) * wide)
+        r_copies[t].wait()
+        done = acc_d[own_rows, span].astype(jnp.bfloat16).astype(jnp.float32)
+        total = done * gates[own_rows, 0:1] + mate_in[:, span].astype(jnp.float32)
+        back_out[:, span] = total.astype(jnp.bfloat16)
+        for i in (2, 1, 0):
+            from_rows = pl.ds(pl.multiple_of(peers[i] * 16, 16), 16)
+            copy = pltpu.make_async_remote_copy(
+                src_ref=back_out.at[from_rows, span], dst_ref=back_in.at[n, :, span],
+                send_sem=b_send.at[i, t], recv_sem=b_recv.at[n, t],
+                device_id=z_devs[i], device_id_type=MESH,
+            )
+            copy.start()
+            b_copies.append(copy)
+    for t in range(TILES):
+        span = slice(t * wide, (t + 1) * wide)
+        total = back_out[pl.ds(pl.multiple_of(n * 16, 16), 16), span].astype(jnp.float32)
+        for i in range(3):
+            pltpu.make_async_remote_copy(
+                src_ref=back_in.at[peers[i], :, span], dst_ref=back_in.at[peers[i], :, span],
+                send_sem=b_send.at[i, t], recv_sem=b_recv.at[peers[i], t],
+                device_id=z_devs[i], device_id_type=MESH,
+            ).wait_recv()
+            total = total + back_in[peers[i], :, span].astype(jnp.float32)
+        final[0, :, span] = total[:8]
+        final[1, :, span] = total[8:]
+    quarter = wd.shape[1] // 2
+    last_out[...] = jnp.concatenate(
+        [final[1 - e, :, :quarter], final[1 - e, :, quarter:]], axis=0
+    ).astype(jnp.bfloat16)
+    f_copy = pltpu.make_async_remote_copy(
+        src_ref=last_out, dst_ref=last_in, send_sem=f_sem.at[0], recv_sem=f_sem.at[1],
+        device_id=x_dev, device_id_type=MESH,
+    )
+    f_copy.start()
+    out_ref[:, pl.ds(pl.multiple_of(e * half, half), half)] = final[e].astype(jnp.bfloat16)
+    f_copy.wait()
+    other = last_in[...].astype(jnp.float32)
+    base = (1 - e) * half
+    out_ref[:, pl.ds(pl.multiple_of(base, quarter), quarter)] = other[:8].astype(jnp.bfloat16)
+    out_ref[:, pl.ds(pl.multiple_of(base + quarter, quarter), quarter)] = other[8:].astype(jnp.bfloat16)
+    for copy in sent + b_copies:
+        copy.wait_send()
+
+
+def fused_device(token_values, block_scales, expert_ids, gate_values, gate_proj, up_proj, down_proj):
+    tok_rows, width = token_values.shape
+    half = width // 2
+    ff = gate_proj.shape[2]
+    total_rows = NODES * 4 * tok_rows
+    column_count = down_proj.shape[2]
+    vmem = pl.BlockSpec(memory_space=pltpu.VMEM)
+    hbm = pl.BlockSpec(memory_space=pl.ANY)
+    bf16, f32 = jnp.bfloat16, jnp.float32
+    dma = pltpu.SemaphoreType.DMA
+    return pl.pallas_call(
+        fused_kernel,
+        out_shape=jax.ShapeDtypeStruct((tok_rows, width), bf16),
+        in_specs=[vmem] * 4 + [hbm] * 3,
+        out_specs=vmem,
+        scratch_shapes=[
+            pltpu.VMEM((width, ff), bf16),
+            pltpu.VMEM((width, ff), bf16),
+            pltpu.VMEM((2 * ff, column_count), bf16),
+            pltpu.VMEM((NODES * 4, 2 * tok_rows, half + 128), bf16),
+            pltpu.VMEM((total_rows, width), bf16),
+            pltpu.VMEM((total_rows, 128), f32),
+            pltpu.VMEM((total_rows, ff), f32),
+            pltpu.VMEM((total_rows, ff), f32),
+            pltpu.VMEM((2, total_rows, ff), bf16),
+            pltpu.VMEM((total_rows, column_count), f32),
+            pltpu.VMEM((total_rows // 2, column_count), bf16),
+            pltpu.VMEM((total_rows // 2, column_count), bf16),
+            pltpu.VMEM((total_rows // 2, column_count), bf16),
+            pltpu.VMEM((NODES, 2 * tok_rows, column_count), bf16),
+            pltpu.VMEM((2, tok_rows, column_count), f32),
+            pltpu.VMEM((2 * tok_rows, column_count // 2), bf16),
+            pltpu.VMEM((2 * tok_rows, column_count // 2), bf16),
+            dma((3,)),
+            dma((NODES * 4, PHASES)),
+            dma((3, PHASES)),
+            dma((4, PHASES)),
+            dma((8, PHASES)),
+            dma((2,)),
+            dma((2, TILES)),
+            dma((3, TILES)),
+            dma((NODES, TILES)),
+            dma((2,)),
+        ],
+        compiler_params=pltpu.CompilerParams(
+            collective_id=1, has_side_effects=True, vmem_limit_bytes=52 * 1024 * 1024
+        ),
+        cost_estimate=pl.CostEstimate(
+            flops=2 * total_rows * width * ff * 3, bytes_accessed=6 * width * ff, transcendentals=0
+        ),
+    )(token_values, block_scales, expert_ids, gate_values, gate_proj, up_proj, down_proj)
+
+
 def solution(mesh):
+    sizes = mesh.shape
+    fits = (sizes["node"], sizes["expert"], sizes["rep"]) == (4, 2, 2)
     return jax.shard_map(
-        per_device,
+        fused_device if fits else per_device,
         mesh=mesh,
         in_specs=(
             P(("parts", "node", "expert", "rep"), None),

time: 109 us -> 45.2 us (0.41)
  Pallas kernels: 0 us -> 41.3 us
  waiting for transfers between devices: 35.8 us -> 0 us
  starting transfers between devices: 19.9 us -> 0 us
  between operations: 13.6 us -> 0.01 us
  matrix products: 13.5 us -> 0 us
  blocking collectives: 11.6 us -> 0 us
  local copies, waits for them, and re-layouts: 11.9 us -> 3.73 us
  other arithmetic: 1.89 us -> 0 us
    pallas_call x0 -> x1, Pallas kernels: none -> 41.3 us  [fused_device(): pl.pallas_call(fused_kernel, out_shape=jax.ShapeDtypeStruct((tok_rows, wi...]
    all_to_all x4 -> x0, waiting for transfers between devices: 28.7 us -> none  [the longest x1 10.6 us: per_device(): lax.all_to_all(outputs.reshape(groups * members, capacity, column_count),...]
    all_to_all x4 -> x0, starting transfers between devices: 19.9 us -> none  [the longest x1 7.25 us: per_device(): lax.all_to_all(spread_gates, ('node', 'expert'), split_axis=0, concat_axi...]
    dot_general x8 -> x0, matrix products: 13.5 us -> none  [the longest x1 4.23 us: per_device(): jnp.dot(lax.all_gather(hidden, 'expert', axis=1, tiled=True), down_local,...]
    all_gather x4 -> x0, blocking collectives: 11.6 us -> none  [the longest x1 5.51 us: per_device(): lax.all_gather(hidden, 'expert', axis=1, tiled=True)]
    reduce_scatter x1 -> x0, waiting for transfers between devices: 7.1 us -> none  [per_device(): lax.psum_scatter(gated_out.astype(jnp.bfloat16), 'rep', scatter_dimension...]
    mul x3 -> x0, local copies, waits for them, and re-layouts: 4.28 us -> none  [the longest x2 4.19 us: dequantize(): values.astype(jnp.float32).reshape(lead_dims + (width // 128, 128))]
    unnamed x4 -> x7, local copies, waits for them, and re-layouts: 0.82 us -> 3.73 us
  transfers between devices with their start and end apart: 5 -> 0, of which waited for: 5 -> 0; matrix products, arithmetic and copies ran while one was open for 6% -> 0% of each run, Pallas kernels for 0% -> 0%
where the time goes in v1:
time: 45.2 us; the launch traced here: 45 us
  Pallas kernels  41.3 us (91%)
  local copies, waits for them, and re-layouts  3.73 us (8%)
    pallas_call x1, Pallas kernels, fused_device(): pl.pallas_call(fused_kernel, out_shape=jax.ShapeDtypeStruct((tok_rows, wi...  41.3 us
    unnamed x7, local copies, waits for them, and re-layouts  3.73 us

profile of v1, /device:TPU:0, one launch (start us, length us, event | category | flops | bytes accessed | tf_op | source)
XLA Modules:
  0.0 45.0 jit_solution(16398212552908001235)
XLA Ops:
  0.0 0.8 %copy.9.gate_ref = bf16[8,4]{1,0:T(8,128)(2,1)S(1)} copy(bf16[8,4]{0,1:T(4,128)(2,1)} %param.10) | data formatting | bytes 128 | tf_op args[3]
  0.8 0.8 %copy.8.ids_ref = s32[8,4]{1,0:T(8,128)S(1)} copy(s32[8,4]{0,1:T(4,128)} %param.9) | data formatting | bytes 256 | tf_op args[2]
  1.5 0.0 copy-start
  1.5 0.9 %copy-done = bf16[8,5120]{1,0:T(8,128)(2,1)S(1)} copy-done((bf16[8,5120]{1,0:T(8,128)(2,1)S(1)}, bf16[8,5120]{1,0:T(8,128)(2,1)}, u32[]{:S(2)}) %copy-start) | copy-done | bytes 81944
  2.4 0.0 copy-start.1
  2.4 0.7 %copy-done.1 = bf16[8,40]{1,0:T(8,128)(2,1)S(1)} copy-done((bf16[8,40]{1,0:T(8,128)(2,1)S(1)}, bf16[8,40]{1,0:T(8,128)(2,1)}, u32[]{:S(2)}) %copy-start.1) | copy-done | bytes 664
  3.1 41.3 %shard_map.73 = bf16[8,5120]{1,0:T(8,128)(2,1)S(1)} custom-call(bf16[8,5120]{1,0:T(8,128)(2,1)S(1)} %copy-done, bf16[8,40]{1,0:T(8,128)(2,1)S(1)} %copy-done.1, s32[8,4]{1,0:T(8,128)S(1)} %copy.8.ids_ref, bf16[8,4]{1,0:T(8,128)(2,1)S(1)} %copy.9.gate_ref, bf16[1,5120,512]{2,1,0:T(8,128)(2,1)} %gate_hbm.1, bf16[1,5120,512]{2,1,0:T(8,128)(2,1)} %up_hbm.1, ...), custom_call_target="tpu_custom_call" | custom-call | flops 2013265920 | bytes 15728640 | tf_op jit(solution)/shard_map/pallas_call | solution.py:340
  44.4 0.6 %copy.11 = bf16[8,5120]{1,0:T(8,128)(2,1)} copy(bf16[8,5120]{1,0:T(8,128)(2,1)S(1)} %shard_map.73) | data formatting | bytes 163840
Async XLA Ops:
  1.5 0.9 %copy-start = (bf16[8,5120]{1,0:T(8,128)(2,1)S(1)}, bf16[8,5120]{1,0:T(8,128)(2,1)}, u32[]{:S(2)}) copy-start(bf16[8,5120]{1,0:T(8,128)(2,1)} %tok_ref.1) | copy-start | bytes 245764
  2.4 0.7 %copy-start.1 = (bf16[8,40]{1,0:T(8,128)(2,1)S(1)}, bf16[8,40]{1,0:T(8,128)(2,1)}, u32[]{:S(2)}) copy-start(bf16[8,40]{1,0:T(8,128)(2,1)} %scale_ref.1) | copy-start | bytes 1924

commit v2 on v1

--- a/solution.py
+++ b/solution.py
@@ -123,16 +123,42 @@
 
 
 NODES = 4
+SLOTS = 8
+USED = 6
+BLOCKS = 3
 MESH = pl.DeviceIdType.MESH
-PHASES = 2
-TILES = 2
+
+
+def by_slots(value):
+    return value.reshape(value.shape[0] // SLOTS, SLOTS, value.shape[1])
+
+
+def pack(value):
+    wide = value.shape[1] // 4
+    spare = by_slots(value[:, 3 * wide:])
+    row = lax.broadcasted_iota(jnp.int32, spare.shape, 1)
+    blocks = []
+    for b in range(BLOCKS):
+        moved = pltpu.roll(spare, USED - 2 * b, 1)
+        kept = by_slots(value[:, b * wide:(b + 1) * wide])
+        blocks.append(jnp.where(row >= USED, moved, kept).reshape(value.shape[0], wide))
+    return blocks
+
+
+def unpack_spare(blocks):
+    threes = [by_slots(block) for block in blocks]
+    row = lax.broadcasted_iota(jnp.int32, threes[0].shape, 1)
+    moved = [pltpu.roll(threes[b], SLOTS - USED + 2 * b, 1) for b in range(BLOCKS)]
+    spare = jnp.where(row < 2, moved[0], jnp.where(row < 4, moved[1], moved[2]))
+    return spare.reshape(blocks[0].shape)
 
 
 def fused_kernel(
-    tok_ref, scale_ref, ids_ref, gate_ref, gate_hbm, up_hbm, down_hbm, out_ref,
-    wg, wu, wd, slabs, rows, gates, acc_g, acc_u, hidden, acc_d,
-    mate_out, mate_in, back_out, back_in, final, last_out, last_in,
-    w_sem, recv_sem, z_sem, x_sem, m_sem, h_sem, r_sem, b_send, b_recv, f_sem,
+    tok_hbm, scale_hbm, ids_hbm, gate_hbm, gate_w_hbm, up_hbm, down_hbm, out_ref,
+    tok_ref, scale_ref, ids_ref, gate_ref,
+    wg, wu, wd, zout, slabs, rows, gates, acc_g, acc_u, hid_out, hid_in, hidden, acc_d,
+    mate_out, mate_in, sums, back_out, back_in, final, last_out, last_in, place, place_in,
+    w_sem, recv_sem, z_sem, x_sem, m_sem, h_sem, r_sem, b_send, b_recv, f_sem, p_sem,
 ):
     part = lax.axis_index("parts")
     n = lax.axis_index("node")
@@ -141,18 +167,26 @@
     width = tok_ref.shape[1]
     half = width // 2
     ff = wg.shape[1]
-    step = half // PHASES
-
+    step = half // 4
+    packed = BLOCKS * step
+    bf16, f32 = jnp.bfloat16, jnp.float32
+
+    small = [
+        pltpu.make_async_copy(src, dst, w_sem.at[3 + i])
+        for i, (src, dst) in enumerate(
+            [(tok_hbm, tok_ref), (scale_hbm, scale_ref), (ids_hbm, ids_ref), (gate_hbm, gate_ref)]
+        )
+    ]
     weights = [
-        pltpu.make_async_copy(gate_hbm.at[0], wg, w_sem.at[0]),
+        pltpu.make_async_copy(gate_w_hbm.at[0], wg, w_sem.at[0]),
         pltpu.make_async_copy(up_hbm.at[0], wu, w_sem.at[1]),
         pltpu.make_async_copy(down_hbm.at[0], wd, w_sem.at[2]),
     ]
-    for copy in weights:
+    for copy in small + weights:
         copy.start()
 
     near = n + 1 - 2 * (n % 2)
-    peers = [near, (n + 2) % 4, 3 - n]
+    peers = [(n + 2) % 4, 3 - n, near]
     z_devs = [(part, p, e, r) for p in peers]
     x_dev = (part, n, 1 - e, r)
     m_dev = (part, n, e, 1 - r)
@@ -165,31 +199,52 @@
         return (a * 2 + b) * 2 + c
 
     me = slot(n, e, r)
-    scales = scale_ref[...].astype(jnp.float32)
-    for j in range(half // 128):
-        lo = tok_ref[:, j * 128:(j + 1) * 128].astype(jnp.float32) * scales[:, j:j + 1]
-        k = j + half // 128
-        hi = tok_ref[:, k * 128:(k + 1) * 128].astype(jnp.float32) * scales[:, k:k + 1]
-        slabs[me, :, j * 128:(j + 1) * 128] = jnp.concatenate([lo, hi], axis=0).astype(jnp.bfloat16)
-    lane = lax.broadcasted_iota(jnp.int32, (tok_ref.shape[0], 128), 1)
-    table = jnp.zeros(lane.shape, jnp.float32)
+    for copy in small:
+        copy.wait()
+    lane = lax.broadcasted_iota(jnp.int32, (SLOTS, 128), 1)
+    table = jnp.zeros(lane.shape, f32)
+    hit = jnp.zeros(lane.shape, f32)
     for k in range(ids_ref.shape[1]):
-        table = table + jnp.where(
-            ids_ref[:, k:k + 1] == lane, gate_ref[:, k:k + 1].astype(jnp.float32), 0.0
-        )
-    slabs[me, :, half:half + 128] = jnp.concatenate([table, table], axis=0).astype(jnp.bfloat16)
+        chosen = ids_ref[:, k:k + 1]
+        table = table + jnp.where(chosen == lane, gate_ref[:, k:k + 1].astype(f32), 0.0)
+        hit = jnp.maximum(hit, jnp.where((chosen >> 1) == (lane >> 3), 1.0, 0.0))
+    row = lax.broadcasted_iota(jnp.int32, lane.shape, 0)
+    ahead = jnp.zeros(lane.shape, f32)
+    for k in range(1, SLOTS):
+        ahead = ahead + jnp.where(row >= k, pltpu.roll(hit, k, 0), 0.0)
+    place[...] = jnp.where(ahead == (lane & 7).astype(f32), hit, 0.0)
+    assign = place[...].T[:NODES * SLOTS].astype(bf16)
+    scales = scale_ref[...].astype(f32)
+    count = half // 128
+    for h in range(2):
+        pieces = [
+            tok_ref[:, j * 128:(j + 1) * 128].astype(f32) * scales[:, j:j + 1]
+            for j in range(h * count, (h + 1) * count)
+        ]
+        values = jnp.concatenate(pieces, axis=1).astype(bf16)
+        placed = jnp.dot(assign, values, preferred_element_type=f32)
+        for b, block in enumerate(pack(placed)):
+            rows[h * 32:(h + 1) * 32, b * step:(b + 1) * step] = block.astype(bf16)
+    slot_gates = jnp.dot(assign, table.astype(bf16), preferred_element_type=f32)
+    for g in range(NODES):
+        at = g * SLOTS
+        for b in range(BLOCKS):
+            span = slice(b * step, (b + 1) * step)
+            lo = rows[0:32, span].astype(f32)[at:at + SLOTS]
+            hi = rows[32:64, span].astype(f32)[at:at + SLOTS]
+            zout[g, :, span] = jnp.concatenate([lo, hi], axis=0).astype(bf16)
+        some = slot_gates[at:at + SLOTS]
+        zout[g, :, packed:packed + 128] = jnp.concatenate([some, some], axis=0).astype(bf16)
 
     pl.semaphore_wait(barrier, 5)
 
     def cols(c):
-        stop = (c + 1) * step + (128 if c == PHASES - 1 else 0)
-        return pl.ds(c * step, stop - c * step)
-
-    def send(src, c, sem, dev):
-        block = slabs.at[src, :, cols(c)]
+        return pl.ds(c * step, step + (128 if c == BLOCKS - 1 else 0))
+
+    def send(src_ref, src, c, sem, dev):
         copy = pltpu.make_async_remote_copy(
-            src_ref=block, dst_ref=block, send_sem=sem, recv_sem=recv_sem.at[src, c],
-            device_id=dev, device_id_type=MESH,
+            src_ref=src_ref.at[:, cols(c)], dst_ref=slabs.at[src, :, cols(c)],
+            send_sem=sem, recv_sem=recv_sem.at[src, c], device_id=dev, device_id_type=MESH,
         )
         copy.start()
         return copy
@@ -201,135 +256,198 @@
             device_id=m_dev, device_id_type=MESH,
         ).wait_recv()
 
+    p_copy = pltpu.make_async_remote_copy(
+        src_ref=place, dst_ref=place_in, send_sem=p_sem.at[0], recv_sem=p_sem.at[1],
+        device_id=x_dev, device_id_type=MESH,
+    )
     sent = []
-    for c in range(PHASES):
-        for i in (2, 1, 0):
-            sent.append(send(me, c, z_sem.at[i, c], z_devs[i]))
-        sent.append(send(me, c, x_sem.at[3, c], x_dev))
-        sent.append(send(me, c, m_sem.at[3, c], m_dev))
-
-    acc_g[...] = jnp.zeros_like(acc_g)
-    acc_u[...] = jnp.zeros_like(acc_u)
-    for c in range(PHASES):
+    for c in range(BLOCKS):
+        for i in range(3):
+            sent.append(send(zout.at[peers[i]], me, c, z_sem.at[i, c], z_devs[i]))
+        sent.append(send(zout.at[n], me, c, x_sem.at[3, c], x_dev))
+        sent.append(send(zout.at[n], me, c, m_sem.at[3, c], m_dev))
+    p_copy.start()
+    slabs[me] = zout[n]
+
+    def pass_z(c):
         for i in range(3):
             src = slot(peers[i], e, r)
             arrive(src, c)
-            sent.append(send(src, c, x_sem.at[i, c], x_dev))
-            sent.append(send(src, c, m_sem.at[i, c], m_dev))
+            sent.append(send(slabs.at[src], src, c, x_sem.at[i, c], x_dev))
+            sent.append(send(slabs.at[src], src, c, m_sem.at[i, c], m_dev))
+
+    def pass_x(c):
         for i, p in enumerate([n] + peers):
             src = slot(p, 1 - e, r)
             arrive(src, c)
-            sent.append(send(src, c, m_sem.at[4 + i, c], m_dev))
+            sent.append(send(slabs.at[src], src, c, m_sem.at[4 + i, c], m_dev))
+
+    pairs = [(rr * NODES + nn, slot(nn, 0, rr), slot(nn, 1, rr)) for rr in range(2) for nn in range(NODES)]
+    acc_g[...] = jnp.zeros_like(acc_g)
+    acc_u[...] = jnp.zeros_like(acc_u)
+
+    def project(first):
+        span = slice(first, first + step)
+        acc_g[...] += jnp.dot(rows[:, span], wg[span, :], preferred_element_type=f32)
+        acc_u[...] += jnp.dot(rows[:, span], wu[span, :], preferred_element_type=f32)
+
+    pass_z(0)
+    for c in range(BLOCKS):
+        pass_x(c)
+        if c + 1 < BLOCKS:
+            pass_z(c + 1)
         for p in [n] + peers:
             arrive(slot(p, e, 1 - r), c)
             arrive(slot(p, 1 - e, 1 - r), c)
-        lo_cols = slice(c * step, (c + 1) * step)
-        hi_cols = slice(half + c * step, half + (c + 1) * step)
-        for rr in range(2):
-            for nn in range(NODES):
-                one = slabs[slot(nn, 0, rr), :, lo_cols].astype(jnp.float32)
-                two = slabs[slot(nn, 1, rr), :, lo_cols].astype(jnp.float32)
-                at = (rr * NODES + nn) * 16
-                rows[at:at + 16, lo_cols] = jnp.concatenate([one[:8], two[:8]], axis=0).astype(jnp.bfloat16)
-                rows[at:at + 16, hi_cols] = jnp.concatenate([one[8:], two[8:]], axis=0).astype(jnp.bfloat16)
+        span = slice(c * step, (c + 1) * step)
+        for at, one, two in pairs:
+            left = slabs[one, :, span].astype(f32)
+            right = slabs[two, :, span].astype(f32)
+            for h in range(2):
+                cut = slice(h * SLOTS, (h + 1) * SLOTS)
+                rows[at * 16:at * 16 + 16, h * half + c * step:h * half + (c + 1) * step] = (
+                    jnp.concatenate([left[cut], right[cut]], axis=0).astype(bf16)
+                )
         if c == 0:
             weights[0].wait()
             weights[1].wait()
-        for span in (lo_cols, hi_cols):
-            acc_g[...] += jnp.dot(rows[:, span], wg[span, :], preferred_element_type=jnp.float32)
-            acc_u[...] += jnp.dot(rows[:, span], wu[span, :], preferred_element_type=jnp.float32)
+        for h in range(2):
+            project(h * half + c * step)
+    for h in range(2):
+        base = h * half
+        for at in range(8):
+            blocks = [
+                rows[at * 16:at * 16 + 16, base + b * step:base + (b + 1) * step].astype(f32)
+                for b in range(BLOCKS)
+            ]
+            rows[at * 16:at * 16 + 16, base + packed:base + half] = unpack_spare(blocks).astype(bf16)
+        project(base + packed)
 
     gate_v = acc_g[...]
-    hidden[e] = ((gate_v / (1.0 + jnp.exp(-gate_v))) * acc_u[...]).astype(jnp.bfloat16)
+    active = (gate_v / (1.0 + jnp.exp(-gate_v))) * acc_u[...]
+    piece = ff // 4
+    for b, block in enumerate(pack(active)):
+        hid_out[:, b * piece:(b + 1) * piece] = block.astype(bf16)
     h_copy = pltpu.make_async_remote_copy(
-        src_ref=hidden.at[e], dst_ref=hidden.at[e], send_sem=h_sem.at[0], recv_sem=h_sem.at[1],
+        src_ref=hid_out, dst_ref=hid_in, send_sem=h_sem.at[0], recv_sem=h_sem.at[1],
         device_id=x_dev, device_id_type=MESH,
     )
     h_copy.start()
+    hidden[...] = active.astype(bf16)
 
     mine = lax.broadcasted_iota(jnp.int32, (16, 128), 1) == n * 2 + r
-    for rr in range(2):
-        for nn in range(NODES):
-            one = slabs[slot(nn, 0, rr), :, half:half + 128].astype(jnp.float32)
-            two = slabs[slot(nn, 1, rr), :, half:half + 128].astype(jnp.float32)
-            both = jnp.concatenate([one[:8], two[:8]], axis=0)
-            at = (rr * NODES + nn) * 16
-            picked = jnp.sum(jnp.where(mine, both, 0.0), axis=1, keepdims=True)
-            gates[at:at + 16, :] = jnp.broadcast_to(picked, (16, 128))
+    for at, one, two in pairs:
+        left = slabs[one, :, packed:packed + 128].astype(f32)
+        right = slabs[two, :, packed:packed + 128].astype(f32)
+        both = jnp.concatenate([left[:SLOTS], right[:SLOTS]], axis=0)
+        picked = jnp.sum(jnp.where(mine, both, 0.0), axis=1, keepdims=True)
+        gates[at * 16:at * 16 + 16, :] = jnp.broadcast_to(picked, (16, 128))
 
     weights[2].wait()
-    wide = wd.shape[1] // TILES
+    tiles = [slice(t * step, (t + 1) * step) for t in (3, 0, 1, 2)]
     own_ff = pl.ds(pl.multiple_of(e * ff, ff), ff)
     other_ff = pl.ds(pl.multiple_of((1 - e) * ff, ff), ff)
-    for t in range(TILES):
-        span = slice(t * wide, (t + 1) * wide)
-        acc_d[:, span] = jnp.dot(hidden[e], wd[own_ff, span], preferred_element_type=jnp.float32)
+    for span in tiles:
+        acc_d[:, span] = jnp.dot(hidden[...], wd[own_ff, span], preferred_element_type=f32)
     h_copy.wait()
+    blocks = [hid_in[:, b * piece:(b + 1) * piece].astype(f32) for b in range(BLOCKS)]
+    hidden[:, :BLOCKS * piece] = hid_in[...]
+    hidden[:, BLOCKS * piece:] = unpack_spare(blocks).astype(bf16)
     group_rows = NODES * 16
     own_rows = pl.ds(pl.multiple_of(r * group_rows, group_rows), group_rows)
     mate_rows = pl.ds(pl.multiple_of((1 - r) * group_rows, group_rows), group_rows)
     r_copies = []
-    for t in range(TILES):
-        span = slice(t * wide, (t + 1) * wide)
-        acc_d[:, span] += jnp.dot(hidden[1 - e], wd[other_ff, span], preferred_element_type=jnp.float32)
-        done = acc_d[mate_rows, span].astype(jnp.bfloat16).astype(jnp.float32)
-        mate_out[:, span] = (done * gates[mate_rows, 0:1]).astype(jnp.bfloat16)
+    b_copies = []
+
+    def give(t):
+        span = tiles[t]
+        acc_d[:, span] += jnp.dot(hidden[...], wd[other_ff, span], preferred_element_type=f32)
+        done = acc_d[mate_rows, span].astype(bf16).astype(f32)
+        mate_out[:, span] = (done * gates[mate_rows, 0:1]).astype(bf16)
         copy = pltpu.make_async_remote_copy(
             src_ref=mate_out.at[:, span], dst_ref=mate_in.at[:, span],
             send_sem=r_sem.at[0, t], recv_sem=r_sem.at[1, t], device_id=m_dev, device_id_type=MESH,
         )
         copy.start()
         r_copies.append(copy)
-    b_copies = []
-    for t in range(TILES):
-        span = slice(t * wide, (t + 1) * wide)
+
+    def take(t):
+        span = tiles[t]
         r_copies[t].wait()
-        done = acc_d[own_rows, span].astype(jnp.bfloat16).astype(jnp.float32)
-        total = done * gates[own_rows, 0:1] + mate_in[:, span].astype(jnp.float32)
-        back_out[:, span] = total.astype(jnp.bfloat16)
-        for i in (2, 1, 0):
+        done = acc_d[own_rows, span].astype(bf16).astype(f32)
+        total = done * gates[own_rows, 0:1] + mate_in[:, span].astype(f32)
+        if t == 0:
+            sums[...] = total
+            return
+        b = t - 1
+        spare = pltpu.roll(by_slots(sums[...]), USED - 2 * b, 1)
+        slots = lax.broadcasted_iota(jnp.int32, spare.shape, 1)
+        mixed = jnp.where(slots >= USED, spare, by_slots(total)).reshape(total.shape)
+        back_out[:, span] = mixed.astype(bf16)
+        for i in range(3):
             from_rows = pl.ds(pl.multiple_of(peers[i] * 16, 16), 16)
             copy = pltpu.make_async_remote_copy(
                 src_ref=back_out.at[from_rows, span], dst_ref=back_in.at[n, :, span],
-                send_sem=b_send.at[i, t], recv_sem=b_recv.at[n, t],
+                send_sem=b_send.at[i, b], recv_sem=b_recv.at[n, b],
                 device_id=z_devs[i], device_id_type=MESH,
             )
             copy.start()
             b_copies.append(copy)
-    for t in range(TILES):
-        span = slice(t * wide, (t + 1) * wide)
-        total = back_out[pl.ds(pl.multiple_of(n * 16, 16), 16), span].astype(jnp.float32)
+
+    give(0)
+    give(1)
+    take(0)
+    give(2)
+    take(1)
+    give(3)
+    take(2)
+    take(3)
+    back_in[n] = back_out[pl.ds(pl.multiple_of(n * 16, 16), 16), :]
+    p_copy.wait()
+    own_lanes = place[...].astype(bf16)[:, :NODES * SLOTS]
+    other_lanes = place_in[...].astype(bf16)[:, :NODES * SLOTS]
+    for b in range(BLOCKS):
+        span = slice(b * step, (b + 1) * step)
         for i in range(3):
+            block = back_in.at[peers[i], :, span]
             pltpu.make_async_remote_copy(
-                src_ref=back_in.at[peers[i], :, span], dst_ref=back_in.at[peers[i], :, span],
-                send_sem=b_send.at[i, t], recv_sem=b_recv.at[peers[i], t],
+                src_ref=block, dst_ref=block,
+                send_sem=b_send.at[i, b], recv_sem=b_recv.at[peers[i], b],
                 device_id=z_devs[i], device_id_type=MESH,
             ).wait_recv()
-            total = total + back_in[peers[i], :, span].astype(jnp.float32)
-        final[0, :, span] = total[:8]
-        final[1, :, span] = total[8:]
-    quarter = wd.shape[1] // 2
-    last_out[...] = jnp.concatenate(
-        [final[1 - e, :, :quarter], final[1 - e, :, quarter:]], axis=0
-    ).astype(jnp.bfloat16)
+    for b in range(BLOCKS):
+        span = slice(b * step, (b + 1) * step)
+        parts = [back_in[g, :, span].astype(f32) for g in range(NODES)]
+        for h in range(2):
+            final[h, :, span] = jnp.concatenate(
+                [value[h * SLOTS:(h + 1) * SLOTS] for value in parts], axis=0
+            )
+    for h in range(2):
+        final[h, :, packed:] = unpack_spare(
+            [final[h, :, b * step:(b + 1) * step] for b in range(BLOCKS)]
+        )
+    theirs = jnp.dot(other_lanes, final[1 - e].astype(bf16), preferred_element_type=f32)
+    quarter = half // 2
+    last_out[...] = jnp.concatenate([theirs[:, :quarter], theirs[:, quarter:]], axis=0).astype(bf16)
     f_copy = pltpu.make_async_remote_copy(
         src_ref=last_out, dst_ref=last_in, send_sem=f_sem.at[0], recv_sem=f_sem.at[1],
         device_id=x_dev, device_id_type=MESH,
     )
     f_copy.start()
-    out_ref[:, pl.ds(pl.multiple_of(e * half, half), half)] = final[e].astype(jnp.bfloat16)
+    ours = jnp.dot(own_lanes, final[e].astype(bf16), preferred_element_type=f32)
+    out_ref[:, pl.ds(pl.multiple_of(e * half, half), half)] = ours.astype(bf16)
     f_copy.wait()
-    other = last_in[...].astype(jnp.float32)
+    other = last_in[...].astype(f32)
     base = (1 - e) * half
-    out_ref[:, pl.ds(pl.multiple_of(base, quarter), quarter)] = other[:8].astype(jnp.bfloat16)
-    out_ref[:, pl.ds(pl.multiple_of(base + quarter, quarter), quarter)] = other[8:].astype(jnp.bfloat16)
+    out_ref[:, pl.ds(pl.multiple_of(base, quarter), quarter)] = other[:SLOTS].astype(bf16)
+    out_ref[:, pl.ds(pl.multiple_of(base + quarter, quarter), quarter)] = other[SLOTS:].astype(bf16)
     for copy in sent + b_copies:
         copy.wait_send()
 
 
 def fused_device(token_values, block_scales, expert_ids, gate_values, gate_proj, up_proj, down_proj):
     tok_rows, width = token_values.shape
-    half = width // 2
+    packed = width // 8 * BLOCKS
     ff = gate_proj.shape[2]
     total_rows = NODES * 4 * tok_rows
     column_count = down_proj.shape[2]
@@ -340,35 +458,46 @@
     return pl.pallas_call(
         fused_kernel,
         out_shape=jax.ShapeDtypeStruct((tok_rows, width), bf16),
-        in_specs=[vmem] * 4 + [hbm] * 3,
+        in_specs=[hbm] * 7,
         out_specs=vmem,
         scratch_shapes=[
+            pltpu.VMEM(token_values.shape, bf16),
+            pltpu.VMEM(block_scales.shape, bf16),
+            pltpu.VMEM(expert_ids.shape, jnp.int32),
+            pltpu.VMEM(gate_values.shape, bf16),
             pltpu.VMEM((width, ff), bf16),
             pltpu.VMEM((width, ff), bf16),
             pltpu.VMEM((2 * ff, column_count), bf16),
-            pltpu.VMEM((NODES * 4, 2 * tok_rows, half + 128), bf16),
+            pltpu.VMEM((NODES, 16, packed + 128), bf16),
+            pltpu.VMEM((NODES * 4, 16, packed + 128), bf16),
             pltpu.VMEM((total_rows, width), bf16),
             pltpu.VMEM((total_rows, 128), f32),
             pltpu.VMEM((total_rows, ff), f32),
             pltpu.VMEM((total_rows, ff), f32),
-            pltpu.VMEM((2, total_rows, ff), bf16),
+            pltpu.VMEM((total_rows, ff // 4 * BLOCKS), bf16),
+            pltpu.VMEM((total_rows, ff // 4 * BLOCKS), bf16),
+            pltpu.VMEM((total_rows, ff), bf16),
             pltpu.VMEM((total_rows, column_count), f32),
             pltpu.VMEM((total_rows // 2, column_count), bf16),
             pltpu.VMEM((total_rows // 2, column_count), bf16),
-            pltpu.VMEM((total_rows // 2, column_count), bf16),
-            pltpu.VMEM((NODES, 2 * tok_rows, column_count), bf16),
-            pltpu.VMEM((2, tok_rows, column_count), f32),
-            pltpu.VMEM((2 * tok_rows, column_count // 2), bf16),
-            pltpu.VMEM((2 * tok_rows, column_count // 2), bf16),
-            dma((3,)),
-            dma((NODES * 4, PHASES)),
-            dma((3, PHASES)),
-            dma((4, PHASES)),
-            dma((8, PHASES)),
+            pltpu.VMEM((total_rows // 2, column_count // 4), f32),
+            pltpu.VMEM((total_rows // 2, packed), bf16),
+            pltpu.VMEM((NODES, 16, packed), bf16),
+            pltpu.VMEM((2, NODES * SLOTS, column_count), f32),
+            pltpu.VMEM((16, column_count // 2), bf16),
+            pltpu.VMEM((16, column_count // 2), bf16),
+            pltpu.VMEM((SLOTS, 128), f32),
+            pltpu.VMEM((SLOTS, 128), f32),
+            dma((7,)),
+            dma((NODES * 4, BLOCKS)),
+            dma((3, BLOCKS)),
+            dma((4, BLOCKS)),
+            dma((8, BLOCKS)),
             dma((2,)),
-            dma((2, TILES)),
-            dma((3, TILES)),
-            dma((NODES, TILES)),
+            dma((2, 4)),
+            dma((3, BLOCKS)),
+            dma((NODES, BLOCKS)),
+            dma((2,)),
             dma((2,)),
         ],
         compiler_params=pltpu.CompilerParams(

time: 45.2 us -> 43.3 us (0.958)
  Pallas kernels: 41.3 us -> 39.4 us
    pallas_call x1, Pallas kernels: 41.3 us -> 39.4 us  [fused_device(): pl.pallas_call(fused_kernel, out_shape=jax.ShapeDtypeStruct((tok_rows, wi...]
where the time goes in v2:
time: 43.3 us; the launch traced here: 43.1 us
  Pallas kernels  39.4 us (91%)
  local copies, waits for them, and re-layouts  3.73 us (9%)
    pallas_call x1, Pallas kernels, fused_device(): pl.pallas_call(fused_kernel, out_shape=jax.ShapeDtypeStruct((tok_rows, wi...  39.4 us
    unnamed x7, local copies, waits for them, and re-layouts  3.73 us

profile of v2, /device:TPU:0, one launch (start us, length us, event | category | flops | bytes accessed | tf_op | source)
XLA Modules:
  0.0 43.1 jit_solution(10718725608585242908)
XLA Ops:
  0.0 0.8 %copy.9.gate_hbm = bf16[8,4]{1,0:T(8,128)(2,1)S(1)} copy(bf16[8,4]{0,1:T(4,128)(2,1)} %param.10) | data formatting | bytes 128 | tf_op args[3]
  0.8 0.8 %copy.8.ids_hbm = s32[8,4]{1,0:T(8,128)S(1)} copy(s32[8,4]{0,1:T(4,128)} %param.9) | data formatting | bytes 256 | tf_op args[2]
  1.5 0.0 copy-start
  1.5 0.9 %copy-done = bf16[8,5120]{1,0:T(8,128)(2,1)S(1)} copy-done((bf16[8,5120]{1,0:T(8,128)(2,1)S(1)}, bf16[8,5120]{1,0:T(8,128)(2,1)}, u32[]{:S(2)}) %copy-start) | copy-done | bytes 81944
  2.4 0.0 copy-start.1
  2.4 0.7 %copy-done.1 = bf16[8,40]{1,0:T(8,128)(2,1)S(1)} copy-done((bf16[8,40]{1,0:T(8,128)(2,1)S(1)}, bf16[8,40]{1,0:T(8,128)(2,1)}, u32[]{:S(2)}) %copy-start.1) | copy-done | bytes 664
  3.1 39.4 %shard_map.73 = bf16[8,5120]{1,0:T(8,128)(2,1)S(1)} custom-call(bf16[8,5120]{1,0:T(8,128)(2,1)S(1)} %copy-done, bf16[8,40]{1,0:T(8,128)(2,1)S(1)} %copy-done.1, s32[8,4]{1,0:T(8,128)S(1)} %copy.8.ids_hbm, bf16[8,4]{1,0:T(8,128)(2,1)S(1)} %copy.9.gate_hbm, bf16[1,5120,512]{2,1,0:T(8,128)(2,1)} %gate_w_hbm.1, bf16[1,5120,512]{2,1,0:T(8,128)(2,1)} %up_hbm.1, ...), custom_call_target="tpu_custom_call" | custom-call | flops 2013265920 | bytes 15728640 | tf_op jit(solution)/shard_map/pallas_call | solution.py:458
  42.5 0.6 %copy.11 = bf16[8,5120]{1,0:T(8,128)(2,1)} copy(bf16[8,5120]{1,0:T(8,128)(2,1)S(1)} %shard_map.73) | data formatting | bytes 163840
Async XLA Ops:
  1.5 0.9 %copy-start = (bf16[8,5120]{1,0:T(8,128)(2,1)S(1)}, bf16[8,5120]{1,0:T(8,128)(2,1)}, u32[]{:S(2)}) copy-start(bf16[8,5120]{1,0:T(8,128)(2,1)} %tok_hbm.1) | copy-start | bytes 245764
  2.4 0.7 %copy-start.1 = (bf16[8,40]{1,0:T(8,128)(2,1)S(1)}, bf16[8,40]{1,0:T(8,128)(2,1)}, u32[]{:S(2)}) copy-start(bf16[8,40]{1,0:T(8,128)(2,1)} %scale_hbm.1) | copy-start | bytes 1924

commit v3 on v2

--- a/solution.py
+++ b/solution.py
@@ -204,11 +204,17 @@
     lane = lax.broadcasted_iota(jnp.int32, (SLOTS, 128), 1)
     table = jnp.zeros(lane.shape, f32)
     hit = jnp.zeros(lane.shape, f32)
-    for k in range(ids_ref.shape[1]):
-        chosen = ids_ref[:, k:k + 1]
-        table = table + jnp.where(chosen == lane, gate_ref[:, k:k + 1].astype(f32), 0.0)
-        hit = jnp.maximum(hit, jnp.where((chosen >> 1) == (lane >> 3), 1.0, 0.0))
     row = lax.broadcasted_iota(jnp.int32, lane.shape, 0)
+    eye = jnp.where(row == lane, 1.0, 0.0)[:, :SLOTS].astype(bf16)
+    turn = (((1,), (1,)), ((), ()))
+    ids_t = lax.dot_general(eye, ids_ref[...].astype(f32).astype(bf16), turn, preferred_element_type=f32)
+    gate_t = lax.dot_general(eye, gate_ref[...], turn, preferred_element_type=f32)
+    lane_f = lane.astype(f32)
+    first_f = ((lane >> 3) * 2).astype(f32)
+    for k in range(ids_ref.shape[0]):
+        chosen = ids_t[:, k:k + 1]
+        table = table + jnp.where(chosen == lane_f, gate_t[:, k:k + 1], 0.0)
+        hit = jnp.maximum(hit, jnp.where((chosen == first_f) | (chosen == first_f + 1.0), 1.0, 0.0))
     ahead = jnp.zeros(lane.shape, f32)
     for k in range(1, SLOTS):
         ahead = ahead + jnp.where(row >= k, pltpu.roll(hit, k, 0), 0.0)
@@ -261,12 +267,20 @@
         device_id=x_dev, device_id_type=MESH,
     )
     sent = []
-    for c in range(BLOCKS):
-        for i in range(3):
-            sent.append(send(zout.at[peers[i]], me, c, z_sem.at[i, c], z_devs[i]))
+    z_sent = []
+
+    def issue(c):
+        z_sent.append(
+            [send(zout.at[peers[i]], me, c, z_sem.at[i, c], z_devs[i]) for i in range(3)]
+        )
         sent.append(send(zout.at[n], me, c, x_sem.at[3, c], x_dev))
         sent.append(send(zout.at[n], me, c, m_sem.at[3, c], m_dev))
-    p_copy.start()
+
+    def drained(c):
+        for copy in z_sent[c]:
+            copy.wait_send()
+
+    issue(0)
     slabs[me] = zout[n]
 
     def pass_z(c):
@@ -291,11 +305,17 @@
         acc_g[...] += jnp.dot(rows[:, span], wg[span, :], preferred_element_type=f32)
         acc_u[...] += jnp.dot(rows[:, span], wu[span, :], preferred_element_type=f32)
 
+    drained(0)
+    issue(1)
     pass_z(0)
+    drained(1)
+    issue(2)
+    p_copy.start()
+    pass_z(1)
     for c in range(BLOCKS):
+        if c == 1:
+            pass_z(2)
         pass_x(c)
-        if c + 1 < BLOCKS:
-            pass_z(c + 1)
         for p in [n] + peers:
             arrive(slot(p, e, 1 - r), c)
             arrive(slot(p, 1 - e, 1 - r), c)
@@ -323,6 +343,7 @@
             rows[at * 16:at * 16 + 16, base + packed:base + half] = unpack_spare(blocks).astype(bf16)
         project(base + packed)
 
+    drained(2)
     gate_v = acc_g[...]
     active = (gate_v / (1.0 + jnp.exp(-gate_v))) * acc_u[...]
     piece = ff // 4
@@ -406,6 +427,22 @@
     p_copy.wait()
     own_lanes = place[...].astype(bf16)[:, :NODES * SLOTS]
     other_lanes = place_in[...].astype(bf16)[:, :NODES * SLOTS]
+    f_copies = []
+
+    def finish(b):
+        span = slice(b * step, (b + 1) * step)
+        theirs = jnp.dot(other_lanes, final[1 - e, :, span].astype(bf16), preferred_element_type=f32)
+        last_out[:, span] = theirs
+        copy = pltpu.make_async_remote_copy(
+            src_ref=last_out.at[:, span], dst_ref=last_in.at[:, span],
+            send_sem=f_sem.at[0, b], recv_sem=f_sem.at[1, b], device_id=x_dev, device_id_type=MESH,
+        )
+        copy.start()
+        f_copies.append(copy)
+        ours = jnp.dot(own_lanes, final[e, :, span].astype(bf16), preferred_element_type=f32)
+        at = pl.multiple_of(e * half + b * step, step)
+        out_ref[:, pl.ds(at, step)] = ours.astype(bf16)
+
     for b in range(BLOCKS):
         span = slice(b * step, (b + 1) * step)
         for i in range(3):
@@ -415,32 +452,21 @@
                 send_sem=b_send.at[i, b], recv_sem=b_recv.at[peers[i], b],
                 device_id=z_devs[i], device_id_type=MESH,
             ).wait_recv()
-    for b in range(BLOCKS):
-        span = slice(b * step, (b + 1) * step)
         parts = [back_in[g, :, span].astype(f32) for g in range(NODES)]
         for h in range(2):
             final[h, :, span] = jnp.concatenate(
                 [value[h * SLOTS:(h + 1) * SLOTS] for value in parts], axis=0
             )
+        finish(b)
     for h in range(2):
         final[h, :, packed:] = unpack_spare(
             [final[h, :, b * step:(b + 1) * step] for b in range(BLOCKS)]
         )
-    theirs = jnp.dot(other_lanes, final[1 - e].astype(bf16), preferred_element_type=f32)
-    quarter = half // 2
-    last_out[...] = jnp.concatenate([theirs[:, :quarter], theirs[:, quarter:]], axis=0).astype(bf16)
-    f_copy = pltpu.make_async_remote_copy(
-        src_ref=last_out, dst_ref=last_in, send_sem=f_sem.at[0], recv_sem=f_sem.at[1],
-        device_id=x_dev, device_id_type=MESH,
-    )
-    f_copy.start()
-    ours = jnp.dot(own_lanes, final[e].astype(bf16), preferred_element_type=f32)
-    out_ref[:, pl.ds(pl.multiple_of(e * half, half), half)] = ours.astype(bf16)
-    f_copy.wait()
-    other = last_in[...].astype(f32)
-    base = (1 - e) * half
-    out_ref[:, pl.ds(pl.multiple_of(base, quarter), quarter)] = other[:SLOTS].astype(bf16)
-    out_ref[:, pl.ds(pl.multiple_of(base + quarter, quarter), quarter)] = other[SLOTS:].astype(bf16)
+    finish(BLOCKS)
+    for b in range(BLOCKS + 1):
+        f_copies[b].wait()
+        at = pl.multiple_of((1 - e) * half + b * step, step)
+        out_ref[:, pl.ds(at, step)] = last_in[:, b * step:(b + 1) * step].astype(bf16)
     for copy in sent + b_copies:
         copy.wait_send()
 
@@ -463,8 +489,8 @@
         scratch_shapes=[
             pltpu.VMEM(token_values.shape, bf16),
             pltpu.VMEM(block_scales.shape, bf16),
-            pltpu.VMEM(expert_ids.shape, jnp.int32),
-            pltpu.VMEM(gate_values.shape, bf16),
+            pltpu.VMEM(expert_ids.shape[::-1], jnp.int32),
+            pltpu.VMEM(gate_values.shape[::-1], bf16),
             pltpu.VMEM((width, ff), bf16),
             pltpu.VMEM((width, ff), bf16),
             pltpu.VMEM((2 * ff, column_count), bf16),
@@ -484,8 +510,8 @@
             pltpu.VMEM((total_rows // 2, packed), bf16),
             pltpu.VMEM((NODES, 16, packed), bf16),
             pltpu.VMEM((2, NODES * SLOTS, column_count), f32),
-            pltpu.VMEM((16, column_count // 2), bf16),
-            pltpu.VMEM((16, column_count // 2), bf16),
+            pltpu.VMEM((SLOTS, column_count), f32),
+            pltpu.VMEM((SLOTS, column_count), f32),
             pltpu.VMEM((SLOTS, 128), f32),
             pltpu.VMEM((SLOTS, 128), f32),
             dma((7,)),
@@ -497,16 +523,16 @@
             dma((2, 4)),
             dma((3, BLOCKS)),
             dma((NODES, BLOCKS)),
-            dma((2,)),
+            dma((2, BLOCKS + 1)),
             dma((2,)),
         ],
         compiler_params=pltpu.CompilerParams(
-            collective_id=1, has_side_effects=True, vmem_limit_bytes=52 * 1024 * 1024
+            collective_id=1, has_side_effects=True, vmem_limit_bytes=60 * 1024 * 1024
         ),
         cost_estimate=pl.CostEstimate(
             flops=2 * total_rows * width * ff * 3, bytes_accessed=6 * width * ff, transcendentals=0
         ),
-    )(token_values, block_scales, expert_ids, gate_values, gate_proj, up_proj, down_proj)
+    )(token_values, block_scales, expert_ids.T, gate_values.T, gate_proj, up_proj, down_proj)
 
 
 def solution(mesh):

time: 43.3 us -> 39.6 us (0.915)
  local copies, waits for them, and re-layouts: 3.73 us -> 1.53 us
  Pallas kernels: 39.4 us -> 37.9 us
    unnamed x7 -> x1, local copies, waits for them, and re-layouts: 3.73 us -> 1.53 us
    pallas_call x1, Pallas kernels: 39.4 us -> 37.9 us  [fused_device(): pl.pallas_call(fused_kernel, out_shape=jax.ShapeDtypeStruct((tok_rows, wi...]
where the time goes in v3:
time: 39.6 us; the launch traced here: 39.4 us
  Pallas kernels  37.9 us (96%)
  local copies, waits for them, and re-layouts  1.53 us (4%)
    pallas_call x1, Pallas kernels, fused_device(): pl.pallas_call(fused_kernel, out_shape=jax.ShapeDtypeStruct((tok_rows, wi...  37.9 us
    unnamed x1, local copies, waits for them, and re-layouts  1.53 us

profile of v3, /device:TPU:0, one launch (start us, length us, event | category | flops | bytes accessed | tf_op | source)
XLA Modules:
  0.0 39.4 jit_solution(3491960771746917772)
XLA Ops:
  0.0 37.9 %shard_map.73 = bf16[8,5120]{1,0:T(8,128)(2,1)} custom-call(bf16[8,5120]{1,0:T(8,128)(2,1)} %tok_hbm.1, bf16[8,40]{1,0:T(8,128)(2,1)} %scale_hbm.1, s32[4,8]{1,0:T(4,128)} %bitcast.2, bf16[4,8]{1,0:T(4,128)(2,1)} %bitcast.3, bf16[1,5120,512]{2,1,0:T(8,128)(2,1)} %gate_w_hbm.1, bf16[1,5120,512]{2,1,0:T(8,128)(2,1)} %up_hbm.1, bf16[1,1024,2560]{2,1,0:T(8,128)(2,1)} %down_hbm.1), custom_call_target="tpu_custom_call" | custom-call | flops 2013265920 | bytes 15728640 | tf_op jit(solution)/shard_map/pallas_call | solution.py:484
  37.9 1.5 %copy.9 = bf16[8,5120]{1,0:T(8,128)(2,1)} copy(bf16[8,5120]{1,0:T(8,128)(2,1)} %shard_map.73) | data formatting | bytes 163840

commit v4 on v3

--- a/solution.py
+++ b/solution.py
@@ -186,7 +186,7 @@
         copy.start()
 
     near = n + 1 - 2 * (n % 2)
-    peers = [(n + 2) % 4, 3 - n, near]
+    peers = [near, (n + 2) % 4, 3 - n]
     z_devs = [(part, p, e, r) for p in peers]
     x_dev = (part, n, 1 - e, r)
     m_dev = (part, n, e, 1 - r)
@@ -305,11 +305,11 @@
         acc_g[...] += jnp.dot(rows[:, span], wg[span, :], preferred_element_type=f32)
         acc_u[...] += jnp.dot(rows[:, span], wu[span, :], preferred_element_type=f32)
 
+    issue(1)
     drained(0)
-    issue(1)
+    issue(2)
     pass_z(0)
     drained(1)
-    issue(2)
     p_copy.start()
     pass_z(1)
     for c in range(BLOCKS):

time: 39.6 us -> 39 us (0.985)
  Pallas kernels: 37.9 us -> 37.3 us
    pallas_call x1, Pallas kernels: 37.9 us -> 37.3 us  [fused_device(): pl.pallas_call(fused_kernel, out_shape=jax.ShapeDtypeStruct((tok_rows, wi...]
where the time goes in v4:
time: 39 us; the launch traced here: 38.9 us
  Pallas kernels  37.3 us (96%)
  local copies, waits for them, and re-layouts  1.53 us (4%)
    pallas_call x1, Pallas kernels, fused_device(): pl.pallas_call(fused_kernel, out_shape=jax.ShapeDtypeStruct((tok_rows, wi...  37.3 us
    unnamed x1, local copies, waits for them, and re-layouts  1.53 us

profile of v4, /device:TPU:0, one launch (start us, length us, event | category | flops | bytes accessed | tf_op | source)
XLA Modules:
  0.0 38.9 jit_solution(2293944880042485528)
XLA Ops:
  0.0 37.3 %shard_map.73 = bf16[8,5120]{1,0:T(8,128)(2,1)} custom-call(bf16[8,5120]{1,0:T(8,128)(2,1)} %tok_hbm.1, bf16[8,40]{1,0:T(8,128)(2,1)} %scale_hbm.1, s32[4,8]{1,0:T(4,128)} %bitcast.2, bf16[4,8]{1,0:T(4,128)(2,1)} %bitcast.3, bf16[1,5120,512]{2,1,0:T(8,128)(2,1)} %gate_w_hbm.1, bf16[1,5120,512]{2,1,0:T(8,128)(2,1)} %up_hbm.1, bf16[1,1024,2560]{2,1,0:T(8,128)(2,1)} %down_hbm.1), custom_call_target="tpu_custom_call" | custom-call | flops 2013265920 | bytes 15728640 | tf_op jit(solution)/shard_map/pallas_call | solution.py:484
  37.3 1.5 %copy.9 = bf16[8,5120]{1,0:T(8,128)(2,1)} copy(bf16[8,5120]{1,0:T(8,128)(2,1)} %shard_map.73) | data formatting | bytes 163840
